TPU v7x, 32 devices: a whole 2x2x4 slice. The times are simulated.
32 devices in a mesh: rot: 4 (over y, core), tile: 4 (over z), nar: 2 (over x).
Axes of the slice: x: 2, y: 2, z: 4, core: 2. Of those that a mesh axis runs over, the one named last changes fastest.
Arguments:
- interp_index: int32 [8, 8, 2, 192, 384], P(None, 'rot', 'nar', 'tile'), may hold values from 0 to 4095
- interp_weight: bfloat16 [8, 8, 2, 192, 384], P(None, 'rot', 'nar', 'tile'), may hold values from 0 to 0.25
- volume: bfloat16 [2, 2, 4, 4096], P(None, 'nar', 'tile'), may hold values from -6 to 6
- spectrum: bfloat16 [2, 4, 2, 192, 384], P(None, 'tile', 'nar'), may hold values from -6 to 6
- ctf_filter: bfloat16 [4, 2, 192, 384], P('tile', 'nar'), may hold values from -1 to 1
- peak_count: int32 [4, 4], P('rot', 'tile'), may hold values from 1 to 4, 9 in all within a row
- peak_orient: int32 [64], P(('rot', 'tile')), may hold values from 0 to 1
- peak_row: int32 [64], P(('rot', 'tile')), may hold values from 0 to 383
- peak_col: int32 [64], P(('rot', 'tile')), may hold values from 0 to 383
- ctf_grid: bfloat16 [32, 2, 18432], P('tile', 'nar'), may hold values from -1 to 1
Outputs:
- peak_max: float32 [4, 2, 73728], P('tile', 'nar')
- peak_mean: float32 [4, 2, 73728], P('tile', 'nar')
- refined: float32 [4, 16, 32], P('rot', None, 'tile')
- best: float32 [4, 16], P('rot')
Inputs may be any that keep to these rules, and one draw needn't show every extreme that they name: `peak_count`: in each orientation group the counts over all tiles sum to 9, and some tile has exactly 4.
All inputs are finite; a program needn't handle non-finite values.
Results may differ from a plain program's by a relative error of at most 0.013.
Values may be sent and summed in bfloat16 or wider, within the bound.
A program may use at most 128 MiB of HBM per device.

v0:
```python
import functools
import math

import jax
import jax.numpy as jnp
import ml_dtypes
import numpy as np
from jax import lax
from jax.experimental import pallas as pl
from jax.experimental.pallas import tpu as pltpu
from jax.sharding import PartitionSpec as P

LANES = 128
SUBL = 8
PACK = 16


def select_tree(items, bits):
    for bit in bits:
        items = [jnp.where(bit, b, a) for a, b in zip(items[::2], items[1::2])]
    return items[0]


def spread_table(table_ref, spread):
    for h in range(spread.shape[1]):
        both = table_ref[:, h * LANES : (h + 1) * LANES].astype(jnp.float32)
        for c in range(2):
            spread[c, h] = jnp.broadcast_to(both[c : c + 1], (SUBL, LANES))


def lookup(spread, index):
    rows = spread.shape[1]
    low = index & (LANES - 1)
    high = index >> 7
    bits = [((high >> b) & 1) == 1 for b in range(rows.bit_length() - 1)]
    return [
        select_tree(
            [
                jnp.take_along_axis(spread[c, h], low, axis=1, mode="promise_in_bounds")
                for h in range(rows)
            ],
            bits,
        )
        for c in range(spread.shape[0])
    ]


def interpolate_block(spread, index_ref, weight_ref, o, r, col):
    parts = []
    weights = [
        weight_ref[k, o, pl.ds(r, PACK), pl.ds(col, LANES)].astype(jnp.float32)
        for k in range(index_ref.shape[0])
    ]
    for s in range(0, PACK, SUBL):
        total = None
        for k in range(index_ref.shape[0]):
            found = lookup(spread, index_ref[k, o, pl.ds(r + s, SUBL), pl.ds(col, LANES)])
            w = weights[k][s : s + SUBL]
            terms = [w * v for v in found]
            total = terms if total is None else [a + b for a, b in zip(total, terms)]
        parts.append(total)
    return [jnp.concatenate([p[c] for p in parts], axis=0) for c in range(2)]


def interpolate_kernel(table_ref, index_ref, weight_ref, out_ref, spread):
    spread_table(table_ref, spread)
    _, orients, rows, columns = index_ref.shape
    per_row = columns // LANES
    blocks = rows // PACK * per_row

    def step(i, carry):
        o, rest = i // blocks, i % blocks
        r = pl.multiple_of(rest // per_row * PACK, PACK)
        col = pl.multiple_of(rest % per_row * LANES, LANES)
        found = interpolate_block(spread, index_ref, weight_ref, o, r, col)
        for c in range(2):
            out_ref[c, o, pl.ds(r, PACK), pl.ds(col, LANES)] = found[c].astype(jnp.bfloat16)
        return carry

    lax.fori_loop(0, orients * blocks, step, 0)


def interpolate(interp_index, interp_weight, table):
    _, orients, _, rows, columns = interp_index.shape
    index, weight = interp_index[:, :, 0], interp_weight[:, :, 0]
    short = -rows % PACK
    if short:
        pad = ((0, 0), (0, 0), (0, short), (0, 0))
        index, weight = jnp.pad(index, pad), jnp.pad(weight, pad)
    vmem = pl.BlockSpec(memory_space=pltpu.VMEM)
    out = pl.pallas_call(
        interpolate_kernel,
        out_shape=jax.ShapeDtypeStruct((2, orients, rows + short, columns), jnp.bfloat16),
        in_specs=[vmem] * 3,
        out_specs=vmem,
        scratch_shapes=[pltpu.VMEM((2, table.shape[1] // LANES, SUBL, LANES), jnp.float32)],
        compiler_params=pltpu.CompilerParams(vmem_limit_bytes=32 * 2**20),
        name="interpolate",
    )(table, index, weight)
    return out[:, :, None, :rows]


def angle(turns, length):
    turns = turns - length * jnp.floor((turns + 0.5) * (1.0 / length))
    turns = jnp.where(turns > 0.5 * length, turns - length, turns)
    x = turns * (2.0 * math.pi / length)
    square = x * x
    cosine = jnp.full_like(x, 1.0 / math.factorial(18) * -1.0)
    sine = jnp.full_like(x, 1.0 / math.factorial(17))
    for p in range(16, -1, -2):
        cosine = cosine * square + (-1.0) ** (p // 2) / math.factorial(p)
    for p in range(15, 0, -2):
        sine = sine * square + (-1.0) ** (p // 2) / math.factorial(p)
    return cosine, sine * x


def push(source, target, send, receive, where):
    return pltpu.make_async_remote_copy(
        src_ref=source,
        dst_ref=target,
        send_sem=send,
        recv_sem=receive,
        device_id=where,
        device_id_type=pl.DeviceIdType.MESH,
    )


def fused_kernel(
    sizes,
    table_hbm, index_hbm, weight_hbm, spec_hbm, filt_hbm, grid_hbm,
    count_hbm, orient_hbm, row_hbm, col_hbm, forward_hbm, back_hbm, bins_hbm,
    top_ref, mean_ref, refined_ref, best_ref,
    table_ref, index_ref, weight_ref, spec_ref, filt_ref, forward, back, bins_ref,
    count_ref, orient_ref, row_ref, col_ref,
    spread, slices, grids, cross, shifted, turn, binned, rows_of, scores,
    sent, held, mine, shared,
    local_sem, slice_send, slice_recv, grid_send, grid_recv, share_send, share_recv,
    half_send, half_recv, map_send, map_recv, score_send, score_recv,
):
    R, T, N = sizes
    r, t, n = lax.axis_index("rot"), lax.axis_index("tile"), lax.axis_index("nar")
    slots = orient_ref.shape[0]
    half, length = filt_ref.shape
    chunks = index_ref.shape[2] // PACK
    orients = index_ref.shape[1]
    blocks = length // LANES
    span = grids.shape[-1]
    f32, bf16 = jnp.float32, jnp.bfloat16

    barrier = pltpu.get_barrier_semaphore()
    across = [(dr, dn) for dn in range(N - 1, -1, -1) for dr in range(R) if dr or dn]
    along = [(dt, dn) for dn in range(N) for dt in range(T) if dt or dn]

    def rot_nar(dr, dn):
        return {"rot": lax.rem(r + dr, R), "tile": t, "nar": lax.rem(n + dn, N)}

    def tile_nar(dt, dn):
        return {"rot": r, "tile": lax.rem(t + dt, T), "nar": lax.rem(n + dn, N)}

    peers = [rot_nar(*d) for d in across] + [tile_nar(*d) for d in along if d[0]]
    for where in peers:
        pl.semaphore_signal(barrier, inc=1, device_id=where, device_id_type=pl.DeviceIdType.MESH)
    quarter = grid_hbm.at[:, pl.ds(pl.multiple_of(r * span, span), span)]
    pairs = dict(
        table=(table_hbm, table_ref),
        spec=(spec_hbm, spec_ref),
        filt=(filt_hbm, filt_ref),
        grid=(quarter, grids.at[r, t]),
        forward=(forward_hbm, forward),
        count=(count_hbm, count_ref),
        orient=(orient_hbm, orient_ref),
        row=(row_hbm, row_ref),
        col=(col_hbm, col_ref),
        bins=(bins_hbm, bins_ref),
        back=(back_hbm, back),
    )
    for o in range(orients):
        pairs[f"index{o}"] = (index_hbm.at[:, o], index_ref.at[:, o])
        pairs[f"weight{o}"] = (weight_hbm.at[:, o], weight_ref.at[:, o])
    first = ["table", "index0", "weight0"]
    order = first + [name for name in pairs if name not in first]
    inputs = {
        name: pltpu.make_async_copy(*pairs[name], local_sem.at[k]) for k, name in enumerate(order)
    }
    for name in order:
        inputs[name].start()
    inputs["table"].wait()
    spread_table(table_ref, spread)
    pl.semaphore_wait(barrier, len(peers))

    def grid_copy(d):
        return push(quarter, grids.at[r, t], grid_send.at[d - 1], grid_recv.at[d - 1], tile_nar(d, 0))

    def share_copy(d):
        return push(grids.at[r], grids.at[r], share_send.at[d - 1], share_recv.at[d - 1], rot_nar(d, 0))

    for d in range(1, T):
        grid_copy(d).start()

    def slice_copy(i, d):
        here = slices.at[t, lax.rem(i, chunks), i // chunks]
        return push(here, here, slice_send.at[i, d - 1], slice_recv.at[i, d - 1], tile_nar(d, 0))

    def half_copy(o, dr, dn):
        k = dn * R + dr - 1
        return push(
            sent.at[o, dn, lax.rem(r + dr, R)], held.at[n, r, o],
            half_send.at[o, k], half_recv.at[o, k], rot_nar(dr, dn),
        )

    def products(o):
        def arrived(i, carry):
            for d in range(1, T):
                there = slices.at[lax.rem(t + T - d, T), lax.rem(i, chunks), i // chunks]
                push(there, there, slice_send.at[i, d - 1], slice_recv.at[i, d - 1], tile_nar(d, 0)).wait_recv()
            return carry

        lax.fori_loop(o * chunks, (o + 1) * chunks, arrived, 0)

        def product(place, carry):
            down = pl.ds(pl.multiple_of(place * PACK, PACK), PACK)
            for b in range(blocks):
                lanes = slice(b * LANES, (b + 1) * LANES)
                mr, mi = (spec_ref[c, down, lanes].astype(f32) for c in range(2))
                filt = filt_ref[down, lanes].astype(f32)
                sr, si = (
                    slices[place // chunks, lax.rem(place, chunks), o, c, :, lanes].astype(f32)
                    for c in range(2)
                )
                cr, ci = filt * sr, filt * si
                cross[o, down, lanes] = (mr * cr + mi * ci).astype(bf16)
                cross[o, down, length + b * LANES : length + (b + 1) * LANES] = (
                    mi * cr - mr * ci
                ).astype(bf16)
            return carry

        lax.fori_loop(0, half // PACK, product, 0)
        for dn in range(N - 1, -1, -1):
            full = lax.dot_general(
                forward[lax.rem(n + dn, N)], cross[o], (((1,), (1,)), ((), ())),
                preferred_element_type=f32,
            ).astype(bf16)
            sent[o, dn] = full.reshape(sent.shape[2:])
            for dr in range(R):
                if dr or dn:
                    half_copy(o, dr, dn).start()
        held[n, r, o] = sent[o, 0, r]

    total = orients * chunks

    def form(i, carry):
        o, j = i // chunks, lax.rem(i, chunks)
        for k in range(orients):
            @pl.when(i == k * chunks)
            def _():
                inputs[f"index{k}"].wait()
                inputs[f"weight{k}"].wait()

        @pl.when(i == 2)
        def _():
            for d in range(1, T):
                grid_copy(d).wait()
            inputs["grid"].wait()
            for d in range(1, R):
                share_copy(d).start()

        @pl.when(i == total - 1)
        def _():
            inputs["spec"].wait()
            inputs["filt"].wait()
            inputs["forward"].wait()
            for k in range(orients - 1):
                products(k)

        def block(b, carry):
            col = pl.multiple_of(b * LANES, LANES)
            start = pl.multiple_of(j * PACK, PACK)
            found = interpolate_block(spread, index_ref, weight_ref, o, start, col)
            for c in range(2):
                slices[t, j, o, c, :, pl.ds(col, LANES)] = found[c].astype(bf16)
            return carry

        lax.fori_loop(0, blocks, block, 0)
        for d in range(1, T):
            slice_copy(i, d).start()
        return carry

    lax.fori_loop(0, total, form, 0)

    for name in ("count", "orient", "row", "col", "bins", "back"):
        inputs[name].wait()
    ky = lax.broadcasted_iota(jnp.int32, (half, LANES), 0) + n * half
    kx = lax.broadcasted_iota(jnp.int32, (PACK, length), 1)
    for i in range(slots):
        c, s = angle((ky * row_ref[i]).astype(f32), length)
        rows_of[0, i], rows_of[1, i] = c, s
        c, s = angle((kx * col_ref[i]).astype(f32), length)
        turn[0, i], turn[1, i] = c, s

    products(orients - 1)

    def peaks(place, carry):
        down = pl.ds(pl.multiple_of(place * PACK, PACK), PACK)
        for b in range(blocks):
            lanes = slice(b * LANES, (b + 1) * LANES)
            mr, mi = (spec_ref[c, down, lanes].astype(f32) for c in range(2))
            plain = []
            for o in range(orients):
                sr, si = (
                    slices[place // chunks, lax.rem(place, chunks), o, c, :, lanes].astype(f32)
                    for c in range(2)
                )
                pr, pi = mr * sr + mi * si, mi * sr - mr * si
                plain.append((pr.astype(bf16).astype(f32), pi.astype(bf16).astype(f32)))
            for i in range(slots):
                pr, pi = plain[0]
                for o in range(1, orients):
                    chosen = orient_ref[i] == o
                    pr = jnp.where(chosen, plain[o][0], pr)
                    pi = jnp.where(chosen, plain[o][1], pi)
                cc, cs = turn[0, i, :, lanes], turn[1, i, :, lanes]
                rc, rs = rows_of[0, i, down, :], rows_of[1, i, down, :]
                value = rc * (pr * cc - pi * cs) - rs * (pr * cs + pi * cc)
                shifted[b, pl.ds(pl.multiple_of(i * half + place * PACK, PACK), PACK), :] = value
        return carry

    lax.fori_loop(0, half // PACK, peaks, 0)
    group = half // 4
    flat = jnp.concatenate(
        [
            jnp.concatenate(
                [
                    shifted[b, pl.ds(i * half + v, group, stride=4), :].astype(bf16)
                    for v in range(4)
                    for b in range(blocks)
                ],
                axis=1,
            )
            for i in range(slots)
        ],
        axis=0,
    )
    flat = jnp.dot(flat, bins_ref[...], preferred_element_type=f32)
    for i in range(slots):
        part = flat[i * group : (i + 1) * group].astype(bf16).astype(f32)
        part = jnp.where(count_ref[0, 0] > i, part, jnp.zeros_like(part))
        for b in range(blocks):
            binned[i, b] = part[:, b * LANES : (b + 1) * LANES]

    for d in range(1, R):
        share_copy(d).wait()
    per = span // length
    defoci = grids.shape[2]

    def assess(m, acc):
        a, within = m // per, lax.rem(m, per)
        for b in range(blocks):
            lanes = pl.ds(pl.multiple_of(within * length + b * LANES, LANES), LANES)
            g = [grids[a, k, :, lanes].astype(f32) for k in range(T)]
            for i in range(slots):
                row = jnp.broadcast_to(
                    binned[i, b, pl.ds(m, 1), :], (defoci, LANES)
                )
                acc = [
                    value + g[k % T] * row if k // T == i else value for k, value in enumerate(acc)
                ]
        return acc

    acc = lax.fori_loop(0, group, assess, [jnp.zeros((defoci, LANES), f32)] * (slots * T))
    lane = lax.broadcasted_iota(jnp.int32, (defoci, LANES), 1)
    for k in range(T):
        mixed = jnp.zeros((defoci, LANES), f32)
        for i in range(slots):
            summed = jnp.sum(acc[i * T + k], axis=1, keepdims=True) * (1.0 / length)
            mixed = jnp.where(lane == t * slots + i, summed, mixed)
        scores[n, t, k * defoci : (k + 1) * defoci, :] = mixed

    def score_copy(k, dt, dn):
        return push(scores.at[n, t], scores.at[n, t], score_send.at[k], score_recv.at[k], tile_nar(dt, dn))

    for k, d in enumerate(along):
        score_copy(k, *d).start()

    rows = held.shape[4]
    parts = []
    for o in range(orients):
        for dr, dn in across:
            there = held.at[lax.rem(n + N - dn, N), lax.rem(r + R - dr, R), o]
            k = dn * R + dr - 1
            push(there, there, half_send.at[o, k], half_recv.at[o, k], rot_nar(dr, dn)).wait_recv()
        corr = None
        for m in range(N):
            for c in range(2):
                part = jnp.dot(
                    held[m, :, o, c].reshape(R * rows, half), back[m, c], preferred_element_type=f32
                )
                corr = part if corr is None else corr + part
        parts += [corr[a * rows : (a + 1) * rows] for a in range(R)]
    top = functools.reduce(jnp.maximum, parts) * (1.0 / length)
    mean = functools.reduce(lambda a, b: a + b, parts) * (1.0 / (length * orients * R))
    shared[r, 0], shared[r, 1] = top.astype(bf16), mean.astype(bf16)
    map_copies = [
        push(shared.at[r], shared.at[r], map_send.at[d - 1], map_recv.at[d - 1], rot_nar(d, 0))
        for d in range(1, R)
    ]
    for copy in map_copies:
        copy.start()

    for k, (dt, dn) in enumerate(along):
        there = scores.at[lax.rem(n + N - dn, N), lax.rem(t + T - dt, T)]
        push(there, there, score_send.at[k], score_recv.at[k], tile_nar(dt, dn)).wait_recv()
    whole = None
    for b in range(T):
        for m in range(N):
            whole = scores[m, b] if whole is None else whole + scores[m, b]
    mine[...] = whole
    listed = T * slots
    best_ref[...] = jnp.max(whole, axis=0, keepdims=True)[:, :listed]
    refined_ref[...] = mine[pl.ds(pl.multiple_of(t * defoci, defoci), defoci), :].T[:listed]

    def left(i, carry):
        for d in range(1, T):
            slice_copy(i, d).wait_send()
        return carry

    lax.fori_loop(0, total, left, 0)
    for o in range(orients):
        for d in across:
            half_copy(o, *d).wait_send()
    for k, d in enumerate(along):
        score_copy(k, *d).wait_send()
    for d in range(1, R):
        there = shared.at[lax.rem(r + R - d, R)]
        push(there, there, map_send.at[d - 1], map_recv.at[d - 1], rot_nar(d, 0)).wait_recv()
    for k, out_ref in enumerate((top_ref, mean_ref)):
        full = jnp.concatenate([shared[a, k].astype(f32) for a in range(R)], axis=0)
        paired = jnp.concatenate([full[:, :half], full[:, half:]], axis=0).T
        for b in range(blocks):
            out_ref[pl.ds(b, half, stride=blocks), :] = paired[:, b * LANES : (b + 1) * LANES]
    for copy in map_copies:
        copy.wait_send()


def constants(length, half, R, N):
    steps = np.arange(length)
    phase = (steps[:, None] * steps[None, :] % length).astype(np.float64) * (2.0 * np.pi / length)
    cosv, sinv = np.cos(phase), np.sin(phase)
    by_x = np.stack([np.concatenate([cosv, -sinv], 0).T, np.concatenate([sinv, cosv], 0).T])
    rows = length // (N * R)
    forward = by_x.reshape(2, N, R, rows, 2 * length).transpose(1, 2, 0, 3, 4)
    forward = forward.reshape(N, R * 2 * rows, 2 * length)
    back = np.stack([cosv, -sinv], 0).reshape(2, N, half, length // 2, 2)
    back = back.transpose(1, 0, 2, 4, 3).reshape(N, 2, half, length)
    bins = np.zeros((4, length, 4, length // 4))
    for v in range(4):
        bins[v, steps, v, steps // 4] = 1.0
    bins = bins.reshape(4 * length, length)
    return [jnp.asarray(a.astype(ml_dtypes.bfloat16)) for a in (forward, back, bins)]


def fused(sizes, args):
    (interp_index, interp_weight, volume, spectrum, ctf_filter, peak_count, peak_orient, peak_row,
     peak_col, ctf_grid) = args
    R, T, N = sizes
    neighbours, orients, _, rows, length = interp_index.shape
    half = spectrum.shape[3]
    slots = peak_orient.shape[0]
    defoci, _, bins_all = ctf_grid.shape
    chunks = rows // PACK
    share = length // (N * R)
    entries = volume.shape[3]
    forward, back, bins = constants(length, half, R, N)
    vmem = pl.BlockSpec(memory_space=pltpu.VMEM)
    hbm = pl.BlockSpec(memory_space=pl.ANY)
    f32, bf16, i32 = jnp.float32, jnp.bfloat16, jnp.int32
    total, peers, near = orients * chunks, R * N - 1, T * N - 1
    listed = T * slots
    dma = pltpu.SemaphoreType.DMA
    flat = length * half // LANES
    top, mean, refined, best = pl.pallas_call(
        functools.partial(fused_kernel, sizes),
        out_shape=(
            jax.ShapeDtypeStruct((flat, LANES), f32),
            jax.ShapeDtypeStruct((flat, LANES), f32),
            jax.ShapeDtypeStruct((listed, defoci), f32),
            jax.ShapeDtypeStruct((1, listed), f32),
        ),
        in_specs=[hbm] * 13,
        out_specs=(vmem,) * 4,
        scratch_shapes=[
            pltpu.VMEM((2, entries), bf16),
            pltpu.VMEM((neighbours, orients, rows, length), i32),
            pltpu.VMEM((neighbours, orients, rows, length), bf16),
            pltpu.VMEM((2, half, length), bf16),
            pltpu.VMEM((half, length), bf16),
            pltpu.VMEM(forward.shape, bf16),
            pltpu.VMEM(back.shape, bf16),
            pltpu.VMEM(bins.shape, bf16),
            pltpu.SMEM((1, 1), i32),
            pltpu.SMEM((slots,), i32),
            pltpu.SMEM((slots,), i32),
            pltpu.SMEM((slots,), i32),
            pltpu.VMEM((2, entries // LANES, SUBL, LANES), f32),
            pltpu.VMEM((T, chunks, orients, 2, PACK, length), bf16),
            pltpu.VMEM((R, T, defoci, bins_all // R), bf16),
            pltpu.VMEM((orients, half, 2 * length), bf16),
            pltpu.VMEM((length // LANES, slots * half, LANES), f32),
            pltpu.VMEM((2, slots, PACK, length), f32),
            pltpu.VMEM((slots, length // LANES, half // 4, LANES), f32),
            pltpu.VMEM((2, slots, half, LANES), f32),
            pltpu.VMEM((N, T, T * defoci, LANES), f32),
            pltpu.VMEM((orients, N, R, 2, share, half), bf16),
            pltpu.VMEM((N, R, orients, 2, share, half), bf16),
            pltpu.VMEM((T * defoci, LANES), f32),
            pltpu.VMEM((R, 2, share, length), bf16),
            dma((11 + 2 * orients,)),
            dma((total, T - 1)), dma((total, T - 1)),
            dma((T - 1,)), dma((T - 1,)),
            dma((R - 1,)), dma((R - 1,)),
            dma((orients, peers)), dma((orients, peers)),
            dma((R - 1,)), dma((R - 1,)),
            dma((near,)), dma((near,)),
        ],
        compiler_params=pltpu.CompilerParams(
            collective_id=0, has_side_effects=True, vmem_limit_bytes=60 * 2**20
        ),
        name="match",
    )(
        volume[:, 0, 0], interp_index[:, :, 0], interp_weight[:, :, 0], spectrum[:, 0, 0],
        ctf_filter[0, 0], ctf_grid[:, 0], peak_count, peak_orient, peak_row, peak_col,
        forward, back, bins,
    )
    return (
        top.reshape(1, 1, -1),
        mean.reshape(1, 1, -1),
        refined.reshape(1, listed, defoci),
        best,
    )


def merged(x, axis, combine):
    everything = jax.tree.map(
        lambda part, kind: lax.all_gather(part.astype(kind), axis), x, (jnp.bfloat16, jnp.bfloat16)
    )

    def take(k):
        return jax.tree.map(lambda part, own: part[k].astype(own.dtype), everything, x)

    return lax.fori_loop(
        1, lax.axis_size(axis), lambda k, so_far: combine(so_far, take(k)), take(0)
    )


def dft_tables(length):
    steps = jnp.arange(length, dtype=jnp.int32)
    phase = (steps[:, None] * steps[None, :] % length).astype(jnp.float32) * (2.0 * jnp.pi / length)
    cosv = jnp.cos(phase).astype(jnp.bfloat16)
    sinv = jnp.sin(phase).astype(jnp.bfloat16)
    wide = jnp.concatenate([jnp.concatenate([cosv, sinv], 1), jnp.concatenate([-sinv, cosv], 1)], 0)
    back = jnp.stack([cosv, -sinv], axis=1)
    return (wide, back)


def combine_stats(first, second):
    return (jnp.maximum(first[0], second[0]), first[1] + second[1])


def shards(
    interp_index,
    interp_weight,
    volume,
    spectrum,
    ctf_filter,
    peak_count,
    peak_orient,
    peak_row,
    peak_col,
    ctf_grid,
):
    table = volume[:, 0, 0]
    weighted = interpolate(interp_index, interp_weight, table)
    length = spectrum.shape[4]
    half = spectrum.shape[3]
    orients = weighted.shape[1]
    slots = peak_orient.shape[0]
    wide, back = dft_tables(length)
    spec = spectrum[:, 0, 0]
    filt = ctf_filter[0, 0]
    piece = lax.all_gather(weighted, "tile", axis=3, tiled=True)
    count = piece.shape[3]
    spec_rows = spec.astype(jnp.float32)
    filt_rows = filt.astype(jnp.float32)
    sr = piece[0, :, 0].astype(jnp.float32)
    si = piece[1, :, 0].astype(jnp.float32)
    cr = filt_rows * sr
    ci = filt_rows * si
    xr = spec_rows[0] * cr + spec_rows[1] * ci
    xi = spec_rows[1] * cr - spec_rows[0] * ci
    cross = jnp.stack([xr, xi], axis=2).astype(jnp.bfloat16)
    rows_out = jnp.dot(
        cross.reshape(orients * count, 2 * length), wide, preferred_element_type=jnp.float32
    )
    rows_out = rows_out.astype(jnp.bfloat16).reshape(orients, count, 2, length)
    picked_r = jnp.take(sr, peak_orient, axis=0)
    picked_i = jnp.take(si, peak_orient, axis=0)
    plain_r = spec_rows[0] * picked_r + spec_rows[1] * picked_i
    plain_i = spec_rows[1] * picked_r - spec_rows[0] * picked_i
    plain = jnp.stack([plain_r, plain_i], axis=2).astype(jnp.bfloat16)
    combined = jnp.concatenate([rows_out, plain], axis=0)
    halfimg = combined[:orients]
    plain = combined[orients:].astype(jnp.float32)
    offset = lax.axis_index("nar") * half
    back_rows = lax.dynamic_slice_in_dim(back, offset, half, 2)
    partial_value = jnp.einsum(
        "yck,okcx->oyx", back_rows, halfimg, preferred_element_type=jnp.float32
    )
    summed = lax.psum_scatter(
        partial_value.astype(jnp.bfloat16), "nar", scatter_dimension=2, tiled=True
    ).astype(jnp.float32)
    corr = summed * (1.0 / length)
    local_max = jnp.max(corr, axis=0)
    local_sum = jnp.sum(corr, axis=0)
    group_count = lax.axis_size("rot")
    top, total = merged((local_max, local_sum), "rot", combine_stats)
    mean = total / (orients * group_count)
    freq_rows = lax.axis_index("nar") * half + jnp.arange(half, dtype=jnp.int32)
    freq_cols = jnp.arange(length, dtype=jnp.int32)
    unit = 2.0 * jnp.pi / length
    row_turn = ((freq_rows[None, :] * peak_row[:, None]) % length).astype(jnp.float32) * unit
    col_turn = ((freq_cols[None, :] * peak_col[:, None]) % length).astype(jnp.float32) * unit
    rc, rs = jnp.cos(row_turn)[:, :, None], jnp.sin(row_turn)[:, :, None]
    cc, cs = jnp.cos(col_turn)[:, None, :], jnp.sin(col_turn)[:, None, :]
    shifted = plain[:, :, 0] * (rc * cc - rs * cs) - plain[:, :, 1] * (rs * cc + rc * cs)
    binned = jnp.sum(shifted.reshape(slots, half, length // 4, 4), axis=3).astype(jnp.bfloat16)
    valid = jnp.arange(slots, dtype=jnp.int32) < peak_count[0, 0]
    binned = jnp.where(valid[:, None, None], binned, jnp.zeros_like(binned)).reshape(slots, -1)
    grid_local = ctf_grid[:, 0]
    grid_count = grid_local.shape[0]
    listed = lax.axis_size("tile") * slots
    part = lax.dot_general(
        lax.all_gather(binned, "tile", axis=0, tiled=True),
        grid_local,
        (((1,), (1,)), ((), ())),
        preferred_element_type=jnp.float32,
    )
    refined = lax.psum(part, "nar") * (1.0 / length)
    best = lax.pmax(jnp.max(refined, axis=1), "tile")
    return (
        top.reshape(1, 1, -1),
        mean.reshape(1, 1, -1),
        refined.reshape(1, listed, grid_count),
        best.reshape(1, listed),
    )


def fits(sizes, args):
    R, T, N = sizes
    _, orients, _, rows, length = args[0].shape
    half, slots, defoci = args[3].shape[3], args[6].shape[0], args[9].shape[0]
    return (
        rows % PACK == 0
        and orients * rows // PACK % 2 == 0
        and T <= 8
        and T * rows == half
        and N * half == length
        and length % LANES == 0
        and length % (N * R * PACK) == 0
        and defoci == SUBL
        and defoci % R == 0
        and T * slots <= LANES
        and length // 4 <= LANES
        and args[9].shape[2] == half * (length // 4)
        and args[9].shape[2] % (R * length) == 0
    )


def solution(mesh):
    sizes = tuple(mesh.shape[axis] for axis in ("rot", "tile", "nar"))

    def body(*args):
        return fused(sizes, args) if fits(sizes, args) else shards(*args)

    return jax.shard_map(
        body,
        mesh=mesh,
        in_specs=(
            P(None, "rot", "nar", "tile", None),
            P(None, "rot", "nar", "tile", None),
            P(None, "nar", "tile", None),
            P(None, "tile", "nar", None, None),
            P("tile", "nar", None, None),
            P("rot", "tile"),
            P(("rot", "tile")),
            P(("rot", "tile")),
            P(("rot", "tile")),
            P("tile", "nar", None),
        ),
        out_specs=(
            P("tile", "nar", None),
            P("tile", "nar", None),
            P("rot", None, "tile"),
            P("rot", None),
        ),
        check_vma=False,
    )
```

profile of v0, /device:TPU:0, one launch (start us, length us, event | category | flops | bytes accessed | tf_op | source)
XLA Modules:
  0.0 54.4 jit_solution(3562775735995229006)
XLA Ops:
  1.3 47.8 %match.1 = (f32[576,128]{1,0:T(8,128)}, f32[576,128]{1,0:T(8,128)}, f32[16,8]{1,0:T(8,128)}, f32[1,16]{1,0:T(1,128)}) custom-call(bf16[2,4096]{1,0:T(2,128)(2,1)} %bitcast.16, s32[8,2,48,384]{3,2,1,0:T(8,128)} %bitcast.9, bf16[8,2,48,384]{3,2,1,0:T(8,128)(2,1)} %bitcast.10, bf16[2,192,384]{2,1,0:T(8,128)(2,1)} %bitcast.11, bf16[192,384]{1,0:T(8,128)(2,1)} %bitcast.15, ...), custom_call_target="tpu_custom_call" | custom-call | tf_op jit(solution)/shard_map/match/pallas_call | solution.py:480
  49.1 0.0 copy-start
  49.1 1.4 %copy.17 = f32[16,8]{0,1:T(8,128)} copy(f32[16,8]{1,0:T(8,128)} %get-tuple-element.10) | data formatting | bytes 1024 | tf_op jit(solution)/shard_map/match/pallas_call | solution.py:480
  50.5 1.7 %copy.22 = f32[1,1,73728]{2,1,0:T(1,128)} copy(f32[1,1,73728]{2,1,0:T(1,128)} %bitcast.14) | data formatting | bytes 589824
  52.2 1.7 %copy.23 = f32[1,1,73728]{2,1,0:T(1,128)} copy(f32[1,1,73728]{2,1,0:T(1,128)} %bitcast.13) | data formatting | bytes 589824
  53.9 0.0 copy-done
  53.9 0.5 copy.24
Async XLA Ops:
  49.1 4.8 %copy-start = (f32[1,16]{1,0:T(1,128)S(1)}, f32[1,16]{1,0:T(1,128)}, u32[]{:S(2)}) copy-start(f32[1,16]{1,0:T(1,128)} %get-tuple-element.19) | copy-start | bytes 196
where the time goes:
time: 55.3 us; the launch traced here: 54.4 us
  Pallas kernels  47.8 us (86%)
  local copies, waits for them, and re-layouts  5.26 us (10%)
  between operations  1.3 us (2%)
    pallas_call x1, Pallas kernels, fused(): pl.pallas_call(functools.partial(fused_kernel, sizes), out_shape=(jax.Sha...  47.8 us
    unnamed x5, local copies, waits for them, and re-layouts  3.9 us
    pallas_call x1, local copies, waits for them, and re-layouts, fused(): pl.pallas_call(functools.partial(fused_kernel, sizes), out_shape=(jax.Sha...  1.36 us

commit v1 on v0

--- a/solution.py
+++ b/solution.py
@@ -21,28 +21,43 @@
     return items[0]
 
 
+def encode(values):
+    rest = jnp.abs(values) * 0.125
+    exponent = jnp.zeros_like(rest)
+    for step in (64, 32, 16, 8, 4, 2, 1):
+        small = rest < 2.0**-step
+        rest = jnp.where(small, rest * 2.0**step, rest)
+        exponent = jnp.where(small, exponent + step, exponent)
+    mantissa = jnp.floor(rest * 256.0)
+    mantissa = jnp.where(values < 0, -mantissa, mantissa)
+    return (mantissa * 128.0 + exponent).astype(jnp.int32)
+
+
+def decode(code):
+    scale = jnp.exp2(-5.0 - (code & 127).astype(jnp.float32))
+    return (code >> 7).astype(jnp.float32) * scale
+
+
 def spread_table(table_ref, spread):
-    for h in range(spread.shape[1]):
-        both = table_ref[:, h * LANES : (h + 1) * LANES].astype(jnp.float32)
-        for c in range(2):
-            spread[c, h] = jnp.broadcast_to(both[c : c + 1], (SUBL, LANES))
+    for h in range(spread.shape[0]):
+        code = encode(table_ref[:, h * LANES : (h + 1) * LANES].astype(jnp.float32))
+        word = code[0:1] * 65536 + (code[1:2] & 65535)
+        spread[h] = jnp.broadcast_to(word, (SUBL, LANES))
 
 
 def lookup(spread, index):
-    rows = spread.shape[1]
+    rows = spread.shape[0]
     low = index & (LANES - 1)
     high = index >> 7
     bits = [((high >> b) & 1) == 1 for b in range(rows.bit_length() - 1)]
-    return [
-        select_tree(
-            [
-                jnp.take_along_axis(spread[c, h], low, axis=1, mode="promise_in_bounds")
-                for h in range(rows)
-            ],
-            bits,
-        )
-        for c in range(spread.shape[0])
-    ]
+    word = select_tree(
+        [
+            jnp.take_along_axis(spread[h], low, axis=1, mode="promise_in_bounds")
+            for h in range(rows)
+        ],
+        bits,
+    )
+    return [decode(word >> 16), decode((word << 16) >> 16)]
 
 
 def interpolate_block(spread, index_ref, weight_ref, o, r, col):
@@ -93,7 +108,7 @@
         out_shape=jax.ShapeDtypeStruct((2, orients, rows + short, columns), jnp.bfloat16),
         in_specs=[vmem] * 3,
         out_specs=vmem,
-        scratch_shapes=[pltpu.VMEM((2, table.shape[1] // LANES, SUBL, LANES), jnp.float32)],
+        scratch_shapes=[pltpu.VMEM((table.shape[1] // LANES, SUBL, LANES), jnp.int32)],
         compiler_params=pltpu.CompilerParams(vmem_limit_bytes=32 * 2**20),
         name="interpolate",
     )(table, index, weight)
@@ -129,7 +144,7 @@
     sizes,
     table_hbm, index_hbm, weight_hbm, spec_hbm, filt_hbm, grid_hbm,
     count_hbm, orient_hbm, row_hbm, col_hbm, forward_hbm, back_hbm, bins_hbm,
-    top_ref, mean_ref, refined_ref, best_ref,
+    top_ref, added_ref, refined_ref, best_ref,
     table_ref, index_ref, weight_ref, spec_ref, filt_ref, forward, back, bins_ref,
     count_ref, orient_ref, row_ref, col_ref,
     spread, slices, grids, cross, shifted, turn, binned, rows_of, scores,
@@ -256,21 +271,13 @@
                 inputs[f"index{k}"].wait()
                 inputs[f"weight{k}"].wait()
 
-        @pl.when(i == 2)
+        @pl.when(i == total - 2)
         def _():
             for d in range(1, T):
                 grid_copy(d).wait()
             inputs["grid"].wait()
             for d in range(1, R):
                 share_copy(d).start()
-
-        @pl.when(i == total - 1)
-        def _():
-            inputs["spec"].wait()
-            inputs["filt"].wait()
-            inputs["forward"].wait()
-            for k in range(orients - 1):
-                products(k)
 
         def block(b, carry):
             col = pl.multiple_of(b * LANES, LANES)
@@ -287,7 +294,7 @@
 
     lax.fori_loop(0, total, form, 0)
 
-    for name in ("count", "orient", "row", "col", "bins", "back"):
+    for name in ("spec", "filt", "forward", "count", "orient", "row", "col", "bins", "back"):
         inputs[name].wait()
     ky = lax.broadcasted_iota(jnp.int32, (half, LANES), 0) + n * half
     kx = lax.broadcasted_iota(jnp.int32, (PACK, length), 1)
@@ -297,7 +304,8 @@
         c, s = angle((kx * col_ref[i]).astype(f32), length)
         turn[0, i], turn[1, i] = c, s
 
-    products(orients - 1)
+    for o in range(orients):
+        products(o)
 
     def peaks(place, carry):
         down = pl.ds(pl.multiple_of(place * PACK, PACK), PACK)
@@ -371,7 +379,7 @@
     for k in range(T):
         mixed = jnp.zeros((defoci, LANES), f32)
         for i in range(slots):
-            summed = jnp.sum(acc[i * T + k], axis=1, keepdims=True) * (1.0 / length)
+            summed = jnp.sum(acc[i * T + k], axis=1, keepdims=True)
             mixed = jnp.where(lane == t * slots + i, summed, mixed)
         scores[n, t, k * defoci : (k + 1) * defoci, :] = mixed
 
@@ -396,9 +404,9 @@
                 )
                 corr = part if corr is None else corr + part
         parts += [corr[a * rows : (a + 1) * rows] for a in range(R)]
-    top = functools.reduce(jnp.maximum, parts) * (1.0 / length)
-    mean = functools.reduce(lambda a, b: a + b, parts) * (1.0 / (length * orients * R))
-    shared[r, 0], shared[r, 1] = top.astype(bf16), mean.astype(bf16)
+    top = functools.reduce(jnp.maximum, parts)
+    added = functools.reduce(lambda a, b: a + b, parts)
+    shared[r, 0], shared[r, 1] = top.astype(bf16), added.astype(bf16)
     map_copies = [
         push(shared.at[r], shared.at[r], map_send.at[d - 1], map_recv.at[d - 1], rot_nar(d, 0))
         for d in range(1, R)
@@ -416,7 +424,7 @@
     mine[...] = whole
     listed = T * slots
     best_ref[...] = jnp.max(whole, axis=0, keepdims=True)[:, :listed]
-    refined_ref[...] = mine[pl.ds(pl.multiple_of(t * defoci, defoci), defoci), :].T[:listed]
+    refined_ref[...] = mine[pl.ds(pl.multiple_of(t * defoci, defoci), defoci), :][:, :listed]
 
     def left(i, carry):
         for d in range(1, T):
@@ -432,7 +440,7 @@
     for d in range(1, R):
         there = shared.at[lax.rem(r + R - d, R)]
         push(there, there, map_send.at[d - 1], map_recv.at[d - 1], rot_nar(d, 0)).wait_recv()
-    for k, out_ref in enumerate((top_ref, mean_ref)):
+    for k, out_ref in enumerate((top_ref, added_ref)):
         full = jnp.concatenate([shared[a, k].astype(f32) for a in range(R)], axis=0)
         paired = jnp.concatenate([full[:, :half], full[:, half:]], axis=0).T
         for b in range(blocks):
@@ -477,12 +485,12 @@
     listed = T * slots
     dma = pltpu.SemaphoreType.DMA
     flat = length * half // LANES
-    top, mean, refined, best = pl.pallas_call(
+    top, added, refined, best = pl.pallas_call(
         functools.partial(fused_kernel, sizes),
         out_shape=(
             jax.ShapeDtypeStruct((flat, LANES), f32),
             jax.ShapeDtypeStruct((flat, LANES), f32),
-            jax.ShapeDtypeStruct((listed, defoci), f32),
+            jax.ShapeDtypeStruct((defoci, listed), f32),
             jax.ShapeDtypeStruct((1, listed), f32),
         ),
         in_specs=[hbm] * 13,
@@ -500,7 +508,7 @@
             pltpu.SMEM((slots,), i32),
             pltpu.SMEM((slots,), i32),
             pltpu.SMEM((slots,), i32),
-            pltpu.VMEM((2, entries // LANES, SUBL, LANES), f32),
+            pltpu.VMEM((entries // LANES, SUBL, LANES), i32),
             pltpu.VMEM((T, chunks, orients, 2, PACK, length), bf16),
             pltpu.VMEM((R, T, defoci, bins_all // R), bf16),
             pltpu.VMEM((orients, half, 2 * length), bf16),
@@ -531,10 +539,10 @@
         forward, back, bins,
     )
     return (
-        top.reshape(1, 1, -1),
-        mean.reshape(1, 1, -1),
-        refined.reshape(1, listed, defoci),
-        best,
+        (top * (1.0 / length)).reshape(1, 1, -1),
+        (added * (1.0 / (length * orients * R))).reshape(1, 1, -1),
+        (refined * (1.0 / length)).T.reshape(1, listed, defoci),
+        best * (1.0 / length),
     )
 
 

time: 55.3 us -> 48.4 us (0.88)
  local copies, waits for them, and re-layouts: 5.26 us -> 0.01 us
  Pallas kernels: 47.8 us -> 43.3 us
  other arithmetic: 0 us -> 3.02 us
    pallas_call x1, Pallas kernels: 47.8 us -> 43.3 us  [fused(): pl.pallas_call(functools.partial(fused_kernel, sizes), out_shape=(jax.Sha...]
    unnamed x5 -> x4, local copies, waits for them, and re-layouts: 3.9 us -> 0.01 us
    mul x0 -> x2, other arithmetic: none -> 2.43 us  [the longest x1 1.92 us: fused(): added * (1.0 / (length * orients * R))]
    pallas_call x1 -> x0, local copies, waits for them, and re-layouts: 1.36 us -> none  [fused(): pl.pallas_call(functools.partial(fused_kernel, sizes), out_shape=(jax.Sha...]
    reshape x0 -> x1, other arithmetic: none -> 0.59 us  [fused(): (refined * (1.0 / length)).T.reshape(1, listed, defoci)]
where the time goes in v1:
time: 48.4 us; the launch traced here: 47.7 us
  Pallas kernels  43.3 us (89%)
  other arithmetic  3.02 us (6%)
  between operations  1.31 us (3%)
    pallas_call x1, Pallas kernels, fused(): pl.pallas_call(functools.partial(fused_kernel, sizes), out_shape=(jax.Sha...  43.3 us
    mul x1, other arithmetic, fused(): added * (1.0 / (length * orients * R))  1.92 us

profile of v1, /device:TPU:0, one launch (start us, length us, event | category | flops | bytes accessed | tf_op | source)
XLA Modules:
  0.0 47.7 jit_solution(1652877760166413295)
XLA Ops:
  1.3 43.3 %match.1 = (f32[576,128]{1,0:T(8,128)}, f32[576,128]{1,0:T(8,128)}, f32[8,16]{1,0:T(8,128)}, f32[1,16]{1,0:T(1,128)}) custom-call(bf16[2,4096]{1,0:T(2,128)(2,1)} %bitcast.19, s32[8,2,48,384]{3,2,1,0:T(8,128)} %bitcast.12, bf16[8,2,48,384]{3,2,1,0:T(8,128)(2,1)} %bitcast.13, bf16[2,192,384]{2,1,0:T(8,128)(2,1)} %bitcast.14, bf16[192,384]{1,0:T(8,128)(2,1)} %bitcast.18, ...), custom_call_target="tpu_custom_call" | custom-call | tf_op jit(solution)/shard_map/match/pallas_call | solution.py:488
  44.6 0.0 copy-start.1
  44.6 0.0 copy-start
  44.6 1.9 %broadcast_multiply_fusion = (f32[576,128]{1,0:T(8,128)}, f32[576,128]{1,0:T(8,128)}) fusion(f32[576,128]{1,0:T(8,128)} %get-tuple-element.9, f32[576,128]{1,0:T(8,128)} %get-tuple-element.8), kind=kLoop, calls=%fused_computation | loop fusion | flops 147456 | bytes 1179648 | tf_op jit(solution)/shard_map/mul | solution.py:543
  46.5 0.0 copy-done.1
  46.5 0.5 %broadcast_multiply_fusion.2 = f32[1,16]{1,0:T(1,128)} fusion(f32[1,16]{1,0:T(1,128)S(1)} %copy-done.1), kind=kLoop, calls=%fused_computation.3 | loop fusion | flops 16 | bytes 128 | tf_op jit(solution)/shard_map/mul | solution.py:545
  47.1 0.0 copy-done
  47.1 0.6 %multiply_bitcast_fusion = f32[1,16,8]{1,2,0:T(8,128)} fusion(f32[8,16]{1,0:T(8,128)S(1)} %copy-done), kind=kLoop, calls=%fused_computation.2 | loop fusion | flops 128 | bytes 1024 | tf_op jit(solution)/shard_map/reshape | solution.py:544
Async XLA Ops:
  44.6 1.9 %copy-start.1 = (f32[1,16]{1,0:T(1,128)S(1)}, f32[1,16]{1,0:T(1,128)}, u32[]{:S(2)}) copy-start(f32[1,16]{1,0:T(1,128)} %get-tuple-element.11) | copy-start | bytes 196
  44.6 2.4 %copy-start = (f32[8,16]{1,0:T(8,128)S(1)}, f32[8,16]{1,0:T(8,128)}, u32[]{:S(2)}) copy-start(f32[8,16]{1,0:T(8,128)} %get-tuple-element.10) | copy-start | bytes 1540

commit v2 on v1

--- a/solution.py
+++ b/solution.py
@@ -206,8 +206,17 @@
     def grid_copy(d):
         return push(quarter, grids.at[r, t], grid_send.at[d - 1], grid_recv.at[d - 1], tile_nar(d, 0))
 
-    def share_copy(d):
-        return push(grids.at[r], grids.at[r], share_send.at[d - 1], share_recv.at[d - 1], rot_nar(d, 0))
+    far = lax.rem(r + 2, R)
+    pair = r + 1 - 2 * lax.rem(r, 2)
+    share_sent = ((r, far), (r, pair), (far, pair))
+    share_found = (far, pair, lax.rem(pair + 2, R))
+
+    def share_copy(k, which, to):
+        here = grids.at[which]
+        return push(here, here, share_send.at[k], share_recv.at[k], {"rot": to, "tile": t, "nar": n})
+
+    def share_arrived(k):
+        share_copy(k, share_found[k], share_sent[k][1]).wait_recv()
 
     for d in range(1, T):
         grid_copy(d).start()
@@ -276,8 +285,8 @@
             for d in range(1, T):
                 grid_copy(d).wait()
             inputs["grid"].wait()
-            for d in range(1, R):
-                share_copy(d).start()
+            for k in range(2):
+                share_copy(k, *share_sent[k]).start()
 
         def block(b, carry):
             col = pl.multiple_of(b * LANES, LANES)
@@ -306,6 +315,8 @@
 
     for o in range(orients):
         products(o)
+    share_arrived(0)
+    share_copy(2, *share_sent[2]).start()
 
     def peaks(place, carry):
         down = pl.ds(pl.multiple_of(place * PACK, PACK), PACK)
@@ -355,8 +366,10 @@
         for b in range(blocks):
             binned[i, b] = part[:, b * LANES : (b + 1) * LANES]
 
-    for d in range(1, R):
-        share_copy(d).wait()
+    for k in range(1, 3):
+        share_arrived(k)
+    for k in range(3):
+        share_copy(k, *share_sent[k]).wait_send()
     per = span // length
     defoci = grids.shape[2]
 
@@ -524,7 +537,7 @@
             dma((11 + 2 * orients,)),
             dma((total, T - 1)), dma((total, T - 1)),
             dma((T - 1,)), dma((T - 1,)),
-            dma((R - 1,)), dma((R - 1,)),
+            dma((3,)), dma((3,)),
             dma((orients, peers)), dma((orients, peers)),
             dma((R - 1,)), dma((R - 1,)),
             dma((near,)), dma((near,)),
@@ -669,6 +682,7 @@
         rows % PACK == 0
         and orients * rows // PACK % 2 == 0
         and T <= 8
+        and R == 4
         and T * rows == half
         and N * half == length
         and length % LANES == 0

time: 48.4 us -> 44.1 us (0.911)
  the two profiles are of different devices: /device:TPU:0 before, /device:TPU:29 now
where the time goes in v2:
time: 44.1 us; the launch traced here: 43.8 us
  Pallas kernels  39.5 us (90%)
  other arithmetic  3.02 us (7%)
  between operations  1.31 us (3%)
    pallas_call x1, Pallas kernels, fused(): pl.pallas_call(functools.partial(fused_kernel, sizes), out_shape=(jax.Sha...  39.5 us
    mul x1, other arithmetic, fused(): added * (1.0 / (length * orients * R))  1.92 us

profile of v2, /device:TPU:29, one launch (start us, length us, event | category | flops | bytes accessed | tf_op | source)
XLA Modules:
  0.0 43.8 jit_solution(16173036132644647611)
XLA Ops:
  1.3 39.5 %match.1 = (f32[576,128]{1,0:T(8,128)}, f32[576,128]{1,0:T(8,128)}, f32[8,16]{1,0:T(8,128)}, f32[1,16]{1,0:T(1,128)}) custom-call(bf16[2,4096]{1,0:T(2,128)(2,1)} %bitcast.19, s32[8,2,48,384]{3,2,1,0:T(8,128)} %bitcast.12, bf16[8,2,48,384]{3,2,1,0:T(8,128)(2,1)} %bitcast.13, bf16[2,192,384]{2,1,0:T(8,128)(2,1)} %bitcast.14, bf16[192,384]{1,0:T(8,128)(2,1)} %bitcast.18, ...), custom_call_target="tpu_custom_call" | custom-call | tf_op jit(solution)/shard_map/match/pallas_call | solution.py:501
  40.8 0.0 copy-start.1
  40.8 0.0 copy-start
  40.8 1.9 %broadcast_multiply_fusion = (f32[576,128]{1,0:T(8,128)}, f32[576,128]{1,0:T(8,128)}) fusion(f32[576,128]{1,0:T(8,128)} %get-tuple-element.9, f32[576,128]{1,0:T(8,128)} %get-tuple-element.8), kind=kLoop, calls=%fused_computation | loop fusion | flops 147456 | bytes 1179648 | tf_op jit(solution)/shard_map/mul | solution.py:556
  42.7 0.0 copy-done.1
  42.7 0.5 %broadcast_multiply_fusion.2 = f32[1,16]{1,0:T(1,128)} fusion(f32[1,16]{1,0:T(1,128)S(1)} %copy-done.1), kind=kLoop, calls=%fused_computation.3 | loop fusion | flops 16 | bytes 128 | tf_op jit(solution)/shard_map/mul | solution.py:558
  43.2 0.0 copy-done
  43.2 0.6 %multiply_bitcast_fusion = f32[1,16,8]{1,2,0:T(8,128)} fusion(f32[8,16]{1,0:T(8,128)S(1)} %copy-done), kind=kLoop, calls=%fused_computation.2 | loop fusion | flops 128 | bytes 1024 | tf_op jit(solution)/shard_map/reshape | solution.py:557
Async XLA Ops:
  40.8 1.9 %copy-start.1 = (f32[1,16]{1,0:T(1,128)S(1)}, f32[1,16]{1,0:T(1,128)}, u32[]{:S(2)}) copy-start(f32[1,16]{1,0:T(1,128)} %get-tuple-element.11) | copy-start | bytes 196
  40.8 2.4 %copy-start = (f32[8,16]{1,0:T(8,128)S(1)}, f32[8,16]{1,0:T(8,128)}, u32[]{:S(2)}) copy-start(f32[8,16]{1,0:T(8,128)} %get-tuple-element.10) | copy-start | bytes 1540

commit v3 on v2

--- a/solution.py
+++ b/solution.py
@@ -366,42 +366,6 @@
         for b in range(blocks):
             binned[i, b] = part[:, b * LANES : (b + 1) * LANES]
 
-    for k in range(1, 3):
-        share_arrived(k)
-    for k in range(3):
-        share_copy(k, *share_sent[k]).wait_send()
-    per = span // length
-    defoci = grids.shape[2]
-
-    def assess(m, acc):
-        a, within = m // per, lax.rem(m, per)
-        for b in range(blocks):
-            lanes = pl.ds(pl.multiple_of(within * length + b * LANES, LANES), LANES)
-            g = [grids[a, k, :, lanes].astype(f32) for k in range(T)]
-            for i in range(slots):
-                row = jnp.broadcast_to(
-                    binned[i, b, pl.ds(m, 1), :], (defoci, LANES)
-                )
-                acc = [
-                    value + g[k % T] * row if k // T == i else value for k, value in enumerate(acc)
-                ]
-        return acc
-
-    acc = lax.fori_loop(0, group, assess, [jnp.zeros((defoci, LANES), f32)] * (slots * T))
-    lane = lax.broadcasted_iota(jnp.int32, (defoci, LANES), 1)
-    for k in range(T):
-        mixed = jnp.zeros((defoci, LANES), f32)
-        for i in range(slots):
-            summed = jnp.sum(acc[i * T + k], axis=1, keepdims=True)
-            mixed = jnp.where(lane == t * slots + i, summed, mixed)
-        scores[n, t, k * defoci : (k + 1) * defoci, :] = mixed
-
-    def score_copy(k, dt, dn):
-        return push(scores.at[n, t], scores.at[n, t], score_send.at[k], score_recv.at[k], tile_nar(dt, dn))
-
-    for k, d in enumerate(along):
-        score_copy(k, *d).start()
-
     rows = held.shape[4]
     parts = []
     for o in range(orients):
@@ -426,6 +390,42 @@
     ]
     for copy in map_copies:
         copy.start()
+
+    for k in range(1, 3):
+        share_arrived(k)
+    for k in range(3):
+        share_copy(k, *share_sent[k]).wait_send()
+    per = span // length
+    defoci = grids.shape[2]
+
+    def assess(m, acc):
+        a, within = m // per, lax.rem(m, per)
+        for b in range(blocks):
+            lanes = pl.ds(pl.multiple_of(within * length + b * LANES, LANES), LANES)
+            g = [grids[a, k, :, lanes].astype(f32) for k in range(T)]
+            for i in range(slots):
+                row = jnp.broadcast_to(
+                    binned[i, b, pl.ds(m, 1), :], (defoci, LANES)
+                )
+                acc = [
+                    value + g[k % T] * row if k // T == i else value for k, value in enumerate(acc)
+                ]
+        return acc
+
+    acc = lax.fori_loop(0, group, assess, [jnp.zeros((defoci, LANES), f32)] * (slots * T))
+    lane = lax.broadcasted_iota(jnp.int32, (defoci, LANES), 1)
+    for k in range(T):
+        mixed = jnp.zeros((defoci, LANES), f32)
+        for i in range(slots):
+            summed = jnp.sum(acc[i * T + k], axis=1, keepdims=True)
+            mixed = jnp.where(lane == t * slots + i, summed, mixed)
+        scores[n, t, k * defoci : (k + 1) * defoci, :] = mixed
+
+    def score_copy(k, dt, dn):
+        return push(scores.at[n, t], scores.at[n, t], score_send.at[k], score_recv.at[k], tile_nar(dt, dn))
+
+    for k, d in enumerate(along):
+        score_copy(k, *d).start()
 
     for k, (dt, dn) in enumerate(along):
         there = scores.at[lax.rem(n + N - dn, N), lax.rem(t + T - dt, T)]

time: 44.1 us -> 48.8 us (1.11)
  the two profiles are of different devices: /device:TPU:29 before, /device:TPU:0 now
where the time goes in v3:
time: 48.8 us; the launch traced here: 48.6 us
  Pallas kernels  44.2 us (91%)
  other arithmetic  3.02 us (6%)
  between operations  1.31 us (3%)
    pallas_call x1, Pallas kernels, fused(): pl.pallas_call(functools.partial(fused_kernel, sizes), out_shape=(jax.Sha...  44.2 us
    mul x1, other arithmetic, fused(): added * (1.0 / (length * orients * R))  1.92 us

profile of v3, /device:TPU:0, one launch (start us, length us, event | category | flops | bytes accessed | tf_op | source)
XLA Modules:
  0.0 48.6 jit_solution(376100342806150445)
XLA Ops:
  1.3 44.2 %match.1 = (f32[576,128]{1,0:T(8,128)}, f32[576,128]{1,0:T(8,128)}, f32[8,16]{1,0:T(8,128)}, f32[1,16]{1,0:T(1,128)}) custom-call(bf16[2,4096]{1,0:T(2,128)(2,1)} %bitcast.19, s32[8,2,48,384]{3,2,1,0:T(8,128)} %bitcast.12, bf16[8,2,48,384]{3,2,1,0:T(8,128)(2,1)} %bitcast.13, bf16[2,192,384]{2,1,0:T(8,128)(2,1)} %bitcast.14, bf16[192,384]{1,0:T(8,128)(2,1)} %bitcast.18, ...), custom_call_target="tpu_custom_call" | custom-call | tf_op jit(solution)/shard_map/match/pallas_call | solution.py:501
  45.5 0.0 copy-start.1
  45.5 0.0 copy-start
  45.5 1.9 %broadcast_multiply_fusion = (f32[576,128]{1,0:T(8,128)}, f32[576,128]{1,0:T(8,128)}) fusion(f32[576,128]{1,0:T(8,128)} %get-tuple-element.9, f32[576,128]{1,0:T(8,128)} %get-tuple-element.8), kind=kLoop, calls=%fused_computation | loop fusion | flops 147456 | bytes 1179648 | tf_op jit(solution)/shard_map/mul | solution.py:556
  47.4 0.0 copy-done.1
  47.4 0.5 %broadcast_multiply_fusion.2 = f32[1,16]{1,0:T(1,128)} fusion(f32[1,16]{1,0:T(1,128)S(1)} %copy-done.1), kind=kLoop, calls=%fused_computation.3 | loop fusion | flops 16 | bytes 128 | tf_op jit(solution)/shard_map/mul | solution.py:558
  48.0 0.0 copy-done
  48.0 0.6 %multiply_bitcast_fusion = f32[1,16,8]{1,2,0:T(8,128)} fusion(f32[8,16]{1,0:T(8,128)S(1)} %copy-done), kind=kLoop, calls=%fused_computation.2 | loop fusion | flops 128 | bytes 1024 | tf_op jit(solution)/shard_map/reshape | solution.py:557
Async XLA Ops:
  45.5 1.9 %copy-start.1 = (f32[1,16]{1,0:T(1,128)S(1)}, f32[1,16]{1,0:T(1,128)}, u32[]{:S(2)}) copy-start(f32[1,16]{1,0:T(1,128)} %get-tuple-element.11) | copy-start | bytes 196
  45.5 2.4 %copy-start = (f32[8,16]{1,0:T(8,128)S(1)}, f32[8,16]{1,0:T(8,128)}, u32[]{:S(2)}) copy-start(f32[8,16]{1,0:T(8,128)} %get-tuple-element.10) | copy-start | bytes 1540
